TPU v7x, 512 devices: a whole 4x4x16 slice. The times are simulated.
512 devices in a mesh: dp: 32 (over z, x_hi), ctx: 16 (over x_lo, y, core).
Axes of the slice: x: 4 (x_hi: 2, x_lo: 2; x = x_hi * 2 + x_lo), y: 4, z: 16, core: 2. Of those that a mesh axis runs over, the one named last changes fastest.
Arguments:
- inputs: bfloat16 [32, 2048, 4096], P('dp', 'ctx'), may hold values from -6 to 6
- letters: int32 [32, 2048], P('dp', 'ctx'), may hold values from 0 to 3
- letter_table: bfloat16 [3, 4, 4096], replicated, may hold values from -3 to 3
- short_taps: bfloat16 [3, 3, 4096], replicated, may hold values from -3 to 3
- residues: float32 [4096, 16], P('ctx'), may hold values from -1.5 to 1.5
- decay_rate: float32 [4096, 16], P('ctx'), may hold values from 2.4414063e-05 to 0.024414062
- cotangent: bfloat16 [32, 2048, 4096], P('dp', 'ctx'), may hold values from -6 to 6
Outputs:
- input_grad: bfloat16 [32, 2048, 4096], P('dp', 'ctx')
- taps_grad: float32 [3, 3, 4096], P(None, None, 'ctx')
- table_grad: float32 [3, 4, 4096], P(None, None, 'ctx')
- residue_grad: float32 [4096, 16], P('ctx')
- decay_grad: float32 [4096, 16], P('ctx')
All inputs are finite; a program needn't handle non-finite values.
Results may differ from a plain program's by a relative error of at most 0.005.
Values may be sent and summed in bfloat16 or wider, within the bound.
A program may use at most 128 MiB of HBM per device.

v0:
```python
import functools

import jax
import jax.numpy as jnp
import numpy as np
from jax import lax
from jax.experimental import pallas as pl
from jax.experimental.pallas import tpu as pltpu
from jax.sharding import PartitionSpec as P

MESH = pl.DeviceIdType.MESH
F32 = jnp.float32
BF16 = jnp.bfloat16
NODES = 16
MODES = 16
ROWS = 16
PIECE = 24
GRADS = 2 * MODES
LANES = 128


def split(values):
    high = values.astype(jnp.bfloat16)
    low = (values - high.astype(np.float64)).astype(jnp.bfloat16)
    return high, low


def tables(span):
    half = span / 2
    centre = (span - 1) / 2
    angles = np.pi * (2 * np.arange(NODES) + 1) / (2 * NODES)
    nodes = centre + half * np.cos(angles)
    places = np.arange(span)
    interp = np.ones((span, NODES))
    for k in range(NODES):
        for other in range(NODES):
            if other != k:
                interp[:, k] *= (places - nodes[other]) / (nodes[k] - nodes[other])
    theta = 2 * np.pi * (np.arange(span) + 0.5) / (2 * span)
    phase = theta[:, None] * places[None, :]
    forward = np.concatenate([np.cos(phase), -np.sin(phase)], axis=0)
    inverse = np.concatenate([np.cos(phase.T), -np.sin(phase.T)], axis=1) / span
    l_hi, l_lo = split(interp)
    w_hi, w_lo = split(forward @ interp)
    m_hi, m_lo = split(interp.T @ inverse)
    return dict(
        nodes=nodes,
        forward=forward.astype(jnp.bfloat16),
        moments=np.concatenate([l_hi.T, l_lo.T], axis=0),
        inverse=np.concatenate([inverse, m_hi.astype(np.float64), m_lo.astype(np.float64)], axis=0).astype(np.float32),
        spread=np.concatenate([l_hi, l_lo], axis=1),
        response=np.concatenate([w_hi, w_lo], axis=1),
    )


def dot(left, right):
    return jnp.dot(left, right, preferred_element_type=F32)


def kernel(n, near, groups, wide, span, chans, nodes, *refs):
    (
        x_hbm, letters_hbm, table_hbm, taps_hbm, res_hbm, decay_hbm, cot_hbm,
        fwd_hbm, mom_hbm, inv_hbm, spread_hbm, resp_hbm, node_hbm,
        grad_hbm, total_ref,
        x_ref, letters_ref, table_ref, taps_ref, res_ref, decay_ref, cot_ref,
        fwd_ref, mom_ref, inv_ref, spread_ref, resp_ref, node_ref,
        x_last, inv_s, grad_ref, xs, key_s, value_s, mix_s, gate_s, conv_s, back_s,
        code_s, hot_t, tab_s, tap_s, spec_m, spec_g, spec_h, prod_s, far_s, fg_s, w_s, tail_s,
        e_s, ep_s, gt_s, gr_s, a_s, r_s, s_s, u_s, al_s, rl_s, row_s, par_s,
        halo_stage, halo_recv, edge_stage, edge_recv,
        hn_stage, hn_recv, pq_stage, pq_recv, fgn_stage, fgn_recv,
        yz_stage, yz_recv, piece_stage, piece_recv,
        mode_stage, mode_one, mode_two, mode_three, tap_near, tap_far,
        in_sem, out_sem, edge_sem,
        hn_send, hn_sem, pq_send, pq_sem, fgn_send, fgn_sem, yz_send, yz_sem, piece_send, piece_sem,
        mo_send, mo_sem, mt_send, mt_sem, mh_send, mh_sem, tn_send, tn_sem, tf_send, tf_sem,
    ) = refs
    me = lax.axis_index("ctx")
    seq = lax.axis_index("dp")
    mine, block = lax.rem(seq, near), seq // near
    ahead, behind = lax.rem(me + 1, n), lax.rem(me + n - 1, n)
    sets = n // wide
    width = wide * chans
    chunks = span // ROWS

    def lanes(d):
        return pl.ds(pl.multiple_of(d * chans, chans), chans)

    def set_lanes(first):
        return pl.ds(pl.multiple_of(first * chans, width), width)

    def first_of(r):
        return lax.rem(me // wide + r, sets) * wide

    def to_ctx(source, target, send, recv, d):
        return pltpu.make_async_remote_copy(
            src_ref=source, dst_ref=target, send_sem=send, recv_sem=recv,
            device_id=(seq, d), device_id_type=MESH,
        )

    def to_dp(source, target, send, recv, p):
        return pltpu.make_async_remote_copy(
            src_ref=source, dst_ref=target, send_sem=send, recv_sem=recv,
            device_id=(p, me), device_id_type=MESH,
        )

    def send_others(first, stage, recv_buffer, send, recv):
        for g in range(wide):
            d = first + g

            @pl.when(d != me)
            def _():
                to_ctx(stage.at[d], recv_buffer.at[me], send.at[d], recv.at[me], d).start()

    def take_others(stage, recv_buffer, send, recv):
        def take(r, carry):
            d = lax.rem(me + r, n)
            to_ctx(stage.at[d], recv_buffer.at[d], send.at[d], recv.at[d], d).wait()
            return carry

        lax.fori_loop(1, n, take, 0)

    barrier = pltpu.get_barrier_semaphore()

    def greet_ctx(r, carry):
        pl.semaphore_signal(barrier, inc=1, device_id=(seq, lax.rem(me + r, n)), device_id_type=MESH)
        return carry

    def greet_near(r, carry):
        peer = block * near + lax.rem(mine + r, near)
        pl.semaphore_signal(barrier, inc=1, device_id=(peer, me), device_id_type=MESH)
        return carry

    def greet_far(r, carry):
        peer = lax.rem(block + r, groups) * near + mine
        pl.semaphore_signal(barrier, inc=1, device_id=(peer, me), device_id_type=MESH)
        return carry

    lax.fori_loop(1, n, greet_ctx, 0)
    lax.fori_loop(1, near, greet_near, 0)
    lax.fori_loop(1, groups, greet_far, 0)

    loads = [
        pltpu.make_async_copy(source, target, in_sem.at[i])
        for i, (source, target) in enumerate([
            (x_hbm.at[pl.ds(span - ROWS, ROWS), :], x_last), (x_hbm, x_ref),
            (letters_hbm, letters_ref), (table_hbm, table_ref), (taps_hbm, taps_ref), (cot_hbm, cot_ref),
            (mom_hbm, mom_ref), (res_hbm, res_ref), (decay_hbm, decay_ref), (node_hbm, node_ref),
            (fwd_hbm, fwd_ref), (inv_hbm, inv_ref), (resp_hbm, resp_ref), (spread_hbm, spread_ref),
        ])
    ]
    for load in loads:
        load.start()
    loads[0].wait()
    halo_stage[...] = x_last[...].astype(F32)[ROWS - 2 :, :]
    pl.semaphore_wait(barrier, (n - 1) + (near - 1) + (groups - 1))
    halo = to_ctx(halo_stage, halo_recv, edge_sem.at[0], edge_sem.at[1], ahead)
    halo.start()
    for load in loads[1:6]:
        load.wait()

    codes = jnp.concatenate([letters_ref[...] + 4 * s for s in range(3)], axis=1)
    hot_t[...] = (lax.broadcasted_iota(jnp.int32, (ROWS, 3 * span), 0) == codes).astype(F32).astype(BF16)
    code_s[...] = jnp.transpose(jnp.broadcast_to(letters_ref[...].astype(F32), (LANES, span)))

    def products(at, which):
        tap = [tap_s[i : i + 1, at] for i in range(9)]
        tab = [tab_s[i : i + 1, at] for i in range(12)]
        for c in which:
            low = c * ROWS
            rows = slice(low, low + ROWS)
            code = code_s[rows, :]
            is_one, is_two, is_three = code == 1.0, code == 2.0, code == 3.0
            lag = [xs[8 + low - j : 8 + low - j + ROWS, at] for j in range(3)]
            stream = []
            for s in range(3):
                part = jnp.where(
                    is_one,
                    tab[4 * s + 1],
                    jnp.where(is_two, tab[4 * s + 2], jnp.where(is_three, tab[4 * s + 3], tab[4 * s])),
                )
                for j in range(3):
                    part = part + tap[3 * s + j] * lag[j]
                stream.append(part)
            key_s[rows, at] = stream[1]
            value_s[rows, at] = stream[2]
            mix_s[rows, at] = (stream[1] * stream[2]).astype(BF16)
            gate_s[rows, at] = (cot_ref[rows, at].astype(F32) * stream[0]).astype(BF16)

    def late_rows(g, carry):
        at = lanes(g)
        xs[8:, at] = x_ref[:, at].astype(F32)
        for s in range(3):
            tap_s[3 * s : 3 * s + 3, at] = taps_ref[s, :, at].astype(F32)
            tab_s[4 * s : 4 * s + 4, at] = table_ref[s, :, at].astype(F32)
        for t in range(chans // LANES):
            products(pl.ds(pl.multiple_of(g * chans + t * LANES, LANES), LANES), range(1, chunks))
        return carry

    lax.fori_loop(0, n, late_rows, 0)
    loads[6].wait()
    halo.wait()
    xs[6:8, :] = jnp.where(me > 0, halo_recv[...], 0.0)

    def node_sums(r, carry):
        first = first_of(r)
        for t in range(width // LANES):
            products(pl.ds(pl.multiple_of(first * chans + t * LANES, LANES), LANES), range(1))
        at = set_lanes(first)
        p_sum = dot(mom_ref[...], mix_s[:, at])
        q_sum = dot(mom_ref[...], gate_s[:, at])
        sums = jnp.concatenate([p_sum[:NODES] + p_sum[NODES:], q_sum[:NODES] + q_sum[NODES:]], axis=0).astype(BF16)
        for g in range(wide):
            pq_stage[first + g] = sums[:, g * chans : (g + 1) * chans]
        send_others(first, pq_stage, pq_recv, pq_send, pq_sem)
        return carry

    lax.fori_loop(1, sets + 1, node_sums, 0)
    pq_recv[me] = pq_stage[me]

    for load in loads[7:]:
        load.wait()
    rate, weight = decay_ref[...], res_ref[...]
    twice = 2.0 * rate
    series = 1.0 - twice * (1.0 / 7.0)
    for term in (6.0, 5.0, 4.0, 3.0, 2.0):
        series = 1.0 - twice * (1.0 / term) * series
    scale = jnp.sqrt(twice * series)
    gain = weight * scale
    par_s[0] = gain
    par_s[1] = scale
    node_col = node_ref[...]
    own_filter = jnp.zeros((NODES, chans), F32)
    for m in range(MODES):
        wave = par_s[0, m : m + 1, :] * jnp.exp(-decay_ref[m : m + 1, :] * node_col)
        gt_s[m] = wave
        own_filter = own_filter + wave
    hn_stage[...] = own_filter.astype(BF16)
    hn_recv[me] = own_filter.astype(BF16)

    def send_filter(r, carry):
        d = lax.rem(me + r, n)
        to_ctx(hn_stage, hn_recv.at[me], hn_send.at[d], hn_sem.at[me], d).start()
        return carry

    lax.fori_loop(1, n, send_filter, 0)
    for m in range(MODES):
        gr_s[m] = par_s[0, m : m + 1, :] * jnp.exp(-decay_ref[m : m + 1, :] * (float(span) - node_col))
    for k in range(NODES):
        e_s[k] = jnp.exp(-rate * float(nodes[k]))
        ep_s[k] = jnp.exp(-rate * float(span - nodes[k]))
    inv_s[...] = inv_ref[...].astype(BF16)

    def spectra(r, carry):
        first = first_of(r)
        at = set_lanes(first)
        spec_m[:, at] = dot(fwd_ref[...], mix_s[:, at])
        spec_g[:, at] = dot(fwd_ref[...], gate_s[:, at])

        def multiply(t, carry):
            some = pl.ds(pl.multiple_of(t * LANES, LANES), LANES)
            here = pl.ds(pl.multiple_of(first * chans + t * LANES, LANES), LANES)
            for c in range(chunks):
                re, im = slice(c * ROWS, c * ROWS + ROWS), slice(span + c * ROWS, span + c * ROWS + ROWS)
                mr, mi = spec_m[re, here], spec_m[im, here]
                gr, gi = spec_g[re, here], spec_g[im, here]
                prod_s[0, re, some] = (gr * mr + gi * mi).astype(BF16)
                prod_s[0, im, some] = (gi * mr - gr * mi).astype(BF16)
            return carry

        lax.fori_loop(0, width // LANES, multiply, 0)
        both = dot(inv_s[span:, :], prod_s[0])
        sums = both[:NODES] + both[NODES:]
        for g in range(wide):
            fgn_stage[first + g] = sums[:, g * chans : (g + 1) * chans]
        send_others(first, fgn_stage, fgn_recv, fgn_send, fgn_sem)
        return carry

    lax.fori_loop(1, sets + 1, spectra, 0)

    take_others(pq_stage, pq_recv, pq_send, pq_sem)

    def states(j, carry):
        row_s[...] = pq_recv[j].astype(F32)
        a_sum = jnp.zeros((MODES, chans), F32)
        r_sum = jnp.zeros((MODES, chans), F32)
        for k in range(NODES):
            a_sum = a_sum + row_s[k : k + 1, :] * ep_s[k]
            r_sum = r_sum + row_s[NODES + k : NODES + k + 1, :] * e_s[k]
        a_s[j] = a_sum
        r_s[j] = r_sum
        return carry

    lax.fori_loop(0, n, states, 0)
    step = jnp.exp(-decay_ref[...] * float(span))

    def recur(i, carry):
        forward_state, backward_state = carry
        s_s[i] = forward_state
        u_s[n - 1 - i] = backward_state
        return step * forward_state + a_s[i], step * backward_state + r_s[n - 1 - i]

    nothing = jnp.zeros((MODES, chans), F32)
    lax.fori_loop(0, n, recur, (nothing, nothing))

    def respond(r, carry):
        d = lax.rem(me + r, n)
        y_sum = jnp.zeros((NODES, chans), F32)
        z_sum = jnp.zeros((NODES, chans), F32)
        for m in range(MODES):
            y_sum = y_sum + s_s[d, m : m + 1, :] * gt_s[m]
            z_sum = z_sum + u_s[d, m : m + 1, :] * gr_s[m]
        yz_stage[d] = jnp.concatenate([y_sum, z_sum], axis=0).astype(BF16)

        @pl.when(r < n)
        def _():
            to_ctx(yz_stage.at[d], yz_recv.at[me], yz_send.at[d], yz_sem.at[me], d).start()

        return carry

    lax.fori_loop(1, n + 1, respond, 0)
    yz_recv[me] = yz_stage[me]

    def take_filter(r, carry):
        d = lax.rem(me + r, n)
        to_ctx(hn_stage, hn_recv.at[d], hn_send.at[d], hn_sem.at[d], d).wait()
        return carry

    lax.fori_loop(1, n, take_filter, 0)

    def inside(r, carry):
        first = first_of(r)
        at = set_lanes(first)
        own = jnp.concatenate([hn_recv[first + g] for g in range(wide)], axis=1)
        spec_h[...] = dot(resp_ref[...], jnp.concatenate([own, own], axis=0))

        def multiply(t, carry):
            some = pl.ds(pl.multiple_of(t * LANES, LANES), LANES)
            here = pl.ds(pl.multiple_of(first * chans + t * LANES, LANES), LANES)
            for c in range(chunks):
                re, im = slice(c * ROWS, c * ROWS + ROWS), slice(span + c * ROWS, span + c * ROWS + ROWS)
                hr, hi = spec_h[re, some], spec_h[im, some]
                mr, mi = spec_m[re, here], spec_m[im, here]
                gr, gi = spec_g[re, here], spec_g[im, here]
                prod_s[0, re, some] = (hr * mr - hi * mi).astype(BF16)
                prod_s[0, im, some] = (hr * mi + hi * mr).astype(BF16)
                prod_s[1, re, some] = (hr * gr + hi * gi).astype(BF16)
                prod_s[1, im, some] = (hr * gi - hi * gr).astype(BF16)
            return carry

        lax.fori_loop(0, width // LANES, multiply, 0)
        conv_s[:, at] = dot(inv_s[:span, :], prod_s[0])
        back_s[:, at] = dot(inv_s[:span, :], prod_s[1])
        return carry

    lax.fori_loop(1, sets + 1, inside, 0)

    def lags(j, carry):
        sums = pq_recv[j].astype(F32)
        row_s[:NODES] = sums[:NODES] * (float(span) - node_ref[...])
        row_s[NODES:] = sums[NODES:] * node_ref[...]
        a_sum = jnp.zeros((MODES, chans), F32)
        r_sum = jnp.zeros((MODES, chans), F32)
        for k in range(NODES):
            a_sum = a_sum + row_s[k : k + 1, :] * ep_s[k]
            r_sum = r_sum + row_s[NODES + k : NODES + k + 1, :] * e_s[k]
        al_s[j] = a_sum
        rl_s[j] = r_sum
        return carry

    lax.fori_loop(0, n, lags, 0)

    def pair(i, carry):
        lag_state, exp_sum, lag_sum = carry
        state, reach = s_s[i], r_s[i]
        exp_sum = exp_sum + reach * state
        lag_sum = lag_sum + rl_s[i] * state + reach * lag_state
        return step * (lag_state + float(span) * state) + al_s[i], exp_sum, lag_sum

    _, exp_sum, lag_sum = lax.fori_loop(0, n, pair, (nothing, nothing, nothing))
    take_others(fgn_stage, fgn_recv, fgn_send, fgn_sem)
    fgn_recv[me] = fgn_stage[me]
    near_sum = fgn_recv[0]
    for d in range(1, n):
        near_sum = near_sum + fgn_recv[d]
    row_s[:NODES] = near_sum
    row_s[NODES:] = near_sum * node_ref[...]
    for k in range(NODES):
        exp_sum = exp_sum + row_s[k : k + 1, :] * e_s[k]
        lag_sum = lag_sum + row_s[NODES + k : NODES + k + 1, :] * e_s[k]
    mode_grads = (
        par_s[1] * exp_sum,
        res_ref[...] * jnp.exp(-2.0 * decay_ref[...]) / par_s[1] * exp_sum - par_s[0] * lag_sum,
    )

    def tile_of(index):
        row, lane = index // (chans // LANES), index % (chans // LANES)
        per = GRADS // 8 * (chans // LANES) // near
        return row // 2, row % 2 * 8, lane * LANES, index // per, index % per * 8

    tiles = range(GRADS // 8 * (chans // LANES))
    for index in tiles:
        which, row, lane, slot, place = tile_of(index)
        mode_stage[slot, place : place + 8, :] = mode_grads[which][row : row + 8, lane : lane + LANES]

    def send_near(source, target, send, recv):
        def one(r, carry):
            p = lax.rem(mine + r, near)
            to_dp(source(p), target.at[mine], send.at[p], recv.at[mine], block * near + p).start()
            return carry

        lax.fori_loop(1, near, one, 0)

    def take_near(target, send, recv):
        def one(r, carry):
            p = lax.rem(mine + r, near)
            to_dp(target.at[p], target.at[p], send.at[p], recv.at[p], block * near + p).wait()
            return carry

        lax.fori_loop(1, near, one, 0)

    def send_far(target, send, recv):
        def one(r, carry):
            b = lax.rem(block + r, groups)
            to_dp(target.at[block], target.at[block], send.at[b], recv.at[block], b * near + mine).start()
            return carry

        lax.fori_loop(1, groups, one, 0)

    def take_far(target, send, recv):
        def one(r, carry):
            b = lax.rem(block + r, groups)
            to_dp(target.at[b], target.at[b], send.at[b], recv.at[b], b * near + mine).wait()
            return carry

        lax.fori_loop(1, groups, one, 0)

    def sum_of(buffer):
        total = buffer[0]
        for p in range(1, buffer.shape[0]):
            total = total + buffer[p]
        return total

    send_near(lambda p: mode_stage.at[p], mode_one, mo_send, mo_sem)
    mode_one[mine] = mode_stage[mine]

    def finish(r, carry):
        first = first_of(r)
        for g in range(wide):
            d = first + g

            @pl.when(d != me)
            def _():
                to_ctx(yz_stage.at[d], yz_recv.at[d], yz_send.at[d], yz_sem.at[d], d).wait()

        y_node = jnp.concatenate([yz_recv[first + g, :NODES] for g in range(wide)], axis=1)
        z_node = jnp.concatenate([yz_recv[first + g, NODES:] for g in range(wide)], axis=1)
        far_s[0] = dot(spread_ref[...], jnp.concatenate([y_node, y_node], axis=0))
        far_s[1] = dot(spread_ref[...], jnp.concatenate([z_node, z_node], axis=0))

        def gradients(g, carry):
            for t in range(chans // LANES):
                some = pl.ds(pl.multiple_of(g * chans + t * LANES, LANES), LANES)
                at = pl.ds(pl.multiple_of((first + g) * chans + t * LANES, LANES), LANES)
                totals = [jnp.zeros((8, LANES), F32) for _ in range(9)]
                for c in range(chunks):
                    low = c * ROWS
                    rows = slice(low, low + ROWS)
                    conv = (conv_s[rows, at] + far_s[0, rows, some]).astype(BF16).astype(F32)
                    back = (back_s[rows, at] + far_s[1, rows, some]).astype(BF16).astype(F32)
                    conv_s[rows, at] = conv
                    back_s[rows, at] = back
                    grads = [
                        cot_ref[rows, at].astype(F32) * conv,
                        back * value_s[rows, at],
                        back * key_s[rows, at],
                    ]
                    lag = [xs[8 + low - j : 8 + low - j + ROWS, at] for j in range(3)]
                    for s in range(3):
                        fg_s[s * span + low : s * span + low + ROWS, some] = grads[s].astype(BF16)
                        for j in range(3):
                            part = grads[s] * lag[j]
                            totals[3 * s + j] = totals[3 * s + j] + (part[:8] + part[8:])
                for i in range(9):
                    piece_stage[first + g, 12 + i : 13 + i, t * LANES : (t + 1) * LANES] = jnp.sum(
                        totals[i], axis=0, keepdims=True
                    )
            return carry

        lax.fori_loop(0, wide, gradients, 0)
        letter_sums = dot(hot_t[...], fg_s[...])
        for g in range(wide):
            piece_stage[first + g, :12, :] = letter_sums[:12, g * chans : (g + 1) * chans]
            piece_stage[first + g, 21:, :] = jnp.zeros((PIECE - 21, chans), F32)
        send_others(first, piece_stage, piece_recv, piece_send, piece_sem)
        return carry

    lax.fori_loop(1, sets + 1, finish, 0)

    take_near(mode_one, mo_send, mo_sem)
    mode_two[block] = sum_of(mode_one)
    send_far(mode_two, mt_send, mt_sem)

    take_others(piece_stage, piece_recv, piece_send, piece_sem)
    piece_recv[me] = piece_stage[me]
    tap_near[mine] = sum_of(piece_recv)
    send_near(lambda p: tap_near.at[mine], tap_near, tn_send, tn_sem)

    w_s[0, span : span + 8, :] = jnp.zeros((8, chans), F32)
    w_s[1, span : span + 8, :] = jnp.zeros((8, chans), F32)

    def input_gradient(d, carry):
        for t in range(chans // LANES):
            some = slice(t * LANES, (t + 1) * LANES)
            at = pl.ds(pl.multiple_of(d * chans + t * LANES, LANES), LANES)
            tap = [tap_s[i : i + 1, at] for i in range(9)]
            for c in reversed(range(chunks)):
                low = c * ROWS
                rows = slice(low, low + ROWS)
                back = back_s[rows, at]
                grads = [cot_ref[rows, at].astype(F32) * conv_s[rows, at], back * value_s[rows, at], back * key_s[rows, at]]
                ahead_by = [tap[j] * grads[0] + tap[3 + j] * grads[1] + tap[6 + j] * grads[2] for j in range(3)]
                w_s[0, rows, some] = ahead_by[1]
                w_s[1, rows, some] = ahead_by[2]
                part = (
                    ahead_by[0]
                    + w_s[0, low + 1 : low + 1 + ROWS, some]
                    + w_s[1, low + 2 : low + 2 + ROWS, some]
                )
                if c < chunks - 1:
                    grad_ref[rows, at] = part.astype(BF16)
                else:
                    tail_s[:, at] = part
            edge_stage[0:1, at] = w_s[1, 0:1, some]
            edge_stage[1:2, at] = w_s[0, 0:1, some] + w_s[1, 1:2, some]
        return carry

    lax.fori_loop(0, n, input_gradient, 0)
    edge = to_ctx(edge_stage, edge_recv, edge_sem.at[2], edge_sem.at[3], behind)
    edge.start()
    body = pl.ds(0, span - ROWS)
    main = pltpu.make_async_copy(grad_ref.at[body, :], grad_hbm.at[body, :], out_sem.at[0])
    main.start()

    take_near(tap_near, tn_send, tn_sem)
    tap_far[block] = sum_of(tap_near)
    send_far(tap_far, tf_send, tf_sem)

    edge.wait()
    tail_s[ROWS - 2 :, :] = tail_s[ROWS - 2 :, :] + jnp.where(me < n - 1, edge_recv[...], 0.0)
    grad_ref[span - ROWS :, :] = tail_s[...].astype(BF16)
    last = pl.ds(span - ROWS, ROWS)
    tail = pltpu.make_async_copy(grad_ref.at[last, :], grad_hbm.at[last, :], out_sem.at[1])
    tail.start()

    take_far(mode_two, mt_send, mt_sem)
    mode_three[mine] = sum_of(mode_two)
    send_near(lambda p: mode_three.at[mine], mode_three, mh_send, mh_sem)
    main.wait()
    tail.wait()
    take_near(mode_three, mh_send, mh_sem)
    for index in tiles:
        which, row, lane, slot, place = tile_of(index)
        row = PIECE + which * MODES + row
        total_ref[row : row + 8, lane : lane + LANES] = mode_three[slot, place : place + 8, :]
    take_far(tap_far, tf_send, tf_sem)
    total_ref[:PIECE, :] = sum_of(tap_far)


def hand_out(total_ref, grad_ref, grad_out, taps_out, table_out, res_out, decay_out):
    grad_out[...] = grad_ref[...]
    for s in range(3):
        table_out[s] = total_ref[4 * s : 4 * s + 4, :]
        taps_out[s] = total_ref[12 + 3 * s : 15 + 3 * s, :]
    res_out[...] = total_ref[PIECE : PIECE + MODES, :]
    decay_out[...] = total_ref[PIECE + MODES :, :]


def shards(n, near, groups, inputs, letters, letter_table, short_taps, residues, decay_rate, cotangent):
    span, width = inputs.shape[1:]
    chans = width // n
    wide = 4 if n % 8 == 0 else 2
    fixed = tables(span)
    nodes = fixed["nodes"]
    node_cols = np.broadcast_to(nodes[:, None], (NODES, chans)).astype(np.float32)
    vmem = pl.BlockSpec(memory_space=pltpu.VMEM)
    anywhere = pl.BlockSpec(memory_space=pl.ANY)
    dma = pltpu.SemaphoreType.DMA
    operands = [inputs[0], letters, letter_table, short_taps, residues.T, decay_rate.T, cotangent[0]] + [
        jnp.asarray(fixed[name]) for name in ("forward", "moments", "inverse", "spread", "response")
    ] + [jnp.asarray(node_cols)]
    several = wide * chans
    share = GRADS * chans // LANES // near
    scratch = [pltpu.VMEM(value.shape, value.dtype) for value in operands] + [
        pltpu.VMEM((ROWS, width), BF16),
        pltpu.VMEM((span + 2 * NODES, 2 * span), BF16),
        pltpu.VMEM((span, width), BF16),
        pltpu.VMEM((span + 8, width), F32),
        pltpu.VMEM((span, width), F32),
        pltpu.VMEM((span, width), F32),
        pltpu.VMEM((span, width), BF16),
        pltpu.VMEM((span, width), BF16),
        pltpu.VMEM((span, width), F32),
        pltpu.VMEM((span, width), F32),
        pltpu.VMEM((span, LANES), F32),
        pltpu.VMEM((ROWS, 3 * span), BF16),
        pltpu.VMEM((ROWS, width), F32),
        pltpu.VMEM((ROWS, width), F32),
        pltpu.VMEM((2 * span, width), F32),
        pltpu.VMEM((2 * span, width), F32),
        pltpu.VMEM((2 * span, several), F32),
        pltpu.VMEM((2, 2 * span, several), BF16),
        pltpu.VMEM((2, span, several), F32),
        pltpu.VMEM((3 * span, several), BF16),
        pltpu.VMEM((2, span + 8, chans), F32),
        pltpu.VMEM((ROWS, width), F32),
    ] + [pltpu.VMEM((NODES, MODES, chans), F32)] * 4 + [pltpu.VMEM((n, MODES, chans), F32)] * 6 + [
        pltpu.VMEM((2 * NODES, chans), F32),
        pltpu.VMEM((2, MODES, chans), F32),
    ] + [pltpu.VMEM((2, width), F32)] * 4 + [
        pltpu.VMEM((NODES, chans), BF16),
        pltpu.VMEM((n, NODES, chans), BF16),
        pltpu.VMEM((n, 2 * NODES, chans), BF16),
        pltpu.VMEM((n, 2 * NODES, chans), BF16),
        pltpu.VMEM((n, NODES, chans), F32),
        pltpu.VMEM((n, NODES, chans), F32),
        pltpu.VMEM((n, 2 * NODES, chans), BF16),
        pltpu.VMEM((n, 2 * NODES, chans), BF16),
        pltpu.VMEM((n, PIECE, chans), F32),
        pltpu.VMEM((n, PIECE, chans), F32),
        pltpu.VMEM((near, share, LANES), F32),
        pltpu.VMEM((near, share, LANES), F32),
        pltpu.VMEM((groups, share, LANES), F32),
        pltpu.VMEM((near, share, LANES), F32),
        pltpu.VMEM((near, PIECE, chans), F32),
        pltpu.VMEM((groups, PIECE, chans), F32),
        dma((len(operands) + 1,)),
        dma((2,)),
        dma((4,)),
    ] + [dma((n,))] * 10 + ([dma((near,))] * 2 + [dma((groups,))] * 2 + [dma((near,))] * 2) + [dma((near,))] * 2 + [dma((groups,))] * 2
    grad, total = pl.pallas_call(
        functools.partial(kernel, n, near, groups, wide, span, chans, nodes),
        out_shape=(
            jax.ShapeDtypeStruct((span, width), BF16),
            jax.ShapeDtypeStruct((PIECE + GRADS, chans), F32),
        ),
        in_specs=[anywhere] * len(operands),
        out_specs=(anywhere, vmem),
        scratch_shapes=scratch,
        compiler_params=pltpu.CompilerParams(
            collective_id=0, has_side_effects=True, vmem_limit_bytes=56 * 1024 * 1024
        ),
    )(*operands)
    grad, taps_grad, table_grad, residue_grad, decay_grad = pl.pallas_call(
        hand_out,
        out_shape=(
            jax.ShapeDtypeStruct((span, width), BF16),
            jax.ShapeDtypeStruct((3, 3, chans), F32),
            jax.ShapeDtypeStruct((3, 4, chans), F32),
            jax.ShapeDtypeStruct((MODES, chans), F32),
            jax.ShapeDtypeStruct((MODES, chans), F32),
        ),
        in_specs=[vmem] * 2,
        out_specs=(vmem,) * 5,
        compiler_params=pltpu.CompilerParams(vmem_limit_bytes=56 * 1024 * 1024),
    )(total, grad)
    return grad[None], taps_grad, table_grad, residue_grad.T, decay_grad.T


def solution(mesh):
    n, sequences = mesh.shape["ctx"], mesh.shape["dp"]
    near = max(k for k in (1, 2, 4, 8) if sequences % k == 0 and k * k <= 2 * sequences)
    in_specs = (
        P("dp", "ctx", None),
        P("dp", "ctx"),
        P(),
        P(),
        P("ctx", None),
        P("ctx", None),
        P("dp", "ctx", None),
    )
    out_specs = (
        P("dp", "ctx", None),
        P(None, None, "ctx"),
        P(None, None, "ctx"),
        P("ctx", None),
        P("ctx", None),
    )
    body = functools.partial(shards, n, near, sequences // near)
    return jax.shard_map(body, mesh=mesh, in_specs=in_specs, out_specs=out_specs, check_vma=False)
```

profile of v0, /device:TPU:1, one launch (start us, length us, event | category | flops | bytes accessed | tf_op | source)
XLA Modules:
  0.0 64.3 jit_solution(5002324831330120847)
XLA Ops:
  0.6 61.4 %shard_map.164 = (bf16[128,4096]{1,0:T(8,128)(2,1)}, f32[56,256]{1,0:T(8,128)}) custom-call(bf16[128,4096]{1,0:T(8,128)(2,1)} %bitcast.7, s32[1,128]{1,0:T(1,128)} %refs_1_.1, bf16[3,4,4096]{2,1,0:T(4,128)(2,1)} %refs_2_.1, bf16[3,3,4096]{2,1,0:T(4,128)(2,1)} %refs_3_.1, f32[16,256]{1,0:T(8,128)} %bitcast.9, f32[16,256]{1,0:T(8,128)} %bitcast.10, ...), custom_call_target="tpu_custom_call" | custom-call | tf_op jit(solution)/shard_map/pallas_call | solution.py:641
  62.0 2.3 %shard_map.165 = (bf16[128,4096]{1,0:T(8,128)(2,1)}, f32[3,3,256]{2,1,0:T(4,128)}, f32[3,4,256]{2,1,0:T(4,128)}, f32[16,256]{1,0:T(8,128)}, f32[16,256]{1,0:T(8,128)}) custom-call(f32[56,256]{1,0:T(8,128)} %get-tuple-element.12.total_ref, bf16[128,4096]{1,0:T(8,128)(2,1)} %get-tuple-element.13.grad_ref), custom_call_target="tpu_custom_call" | custom-call | tf_op jit(solution)/shard_map/pallas_call | solution.py:654
where the time goes:
time: 64.5 us; the launch traced here: 64.3 us
  Pallas kernels  63.7 us (99%)
    pallas_call x1, Pallas kernels, shards(): pl.pallas_call(functools.partial(kernel, n, near, groups, wide, span, cha...  61.4 us
    pallas_call x1, Pallas kernels, shards(): pl.pallas_call(hand_out, out_shape=(jax.ShapeDtypeStruct((span, width), B...  2.31 us

commit v1 on v0

--- a/solution.py
+++ b/solution.py
@@ -53,6 +53,21 @@
     )
 
 
+def packed(rows):
+    half = rows.shape[1] // 2
+    return jnp.concatenate(
+        [rows[:16], jnp.concatenate([rows[16:, :half], rows[16:, half:]], axis=0)], axis=1
+    ).astype(BF16)
+
+
+def unpacked(block):
+    wide = block.shape[1] // 3 * 2
+    block = block.astype(F32)
+    return jnp.concatenate(
+        [block[:, :wide], jnp.concatenate([block[:8, wide:], block[8:, wide:]], axis=1)], axis=0
+    )
+
+
 def dot(left, right):
     return jnp.dot(left, right, preferred_element_type=F32)
 
@@ -65,7 +80,7 @@
         x_ref, letters_ref, table_ref, taps_ref, res_ref, decay_ref, cot_ref,
         fwd_ref, mom_ref, inv_ref, spread_ref, resp_ref, node_ref,
         x_last, inv_s, grad_ref, xs, key_s, value_s, mix_s, gate_s, conv_s, back_s,
-        code_s, hot_t, tab_s, tap_s, spec_m, spec_g, spec_h, prod_s, far_s, fg_s, w_s, tail_s,
+        code_s, hot_t, tab_s, tap_s, spec_m, spec_g, spec_h, prod_s, far_s, fg_s, sums_s, w_s, tail_s,
         e_s, ep_s, gt_s, gr_s, a_s, r_s, s_s, u_s, al_s, rl_s, row_s, par_s,
         halo_stage, halo_recv, edge_stage, edge_recv,
         hn_stage, hn_recv, pq_stage, pq_recv, fgn_stage, fgn_recv,
@@ -120,6 +135,29 @@
 
         lax.fori_loop(1, n, take, 0)
 
+    steps = near // 2
+    along, side = seq // 2, lax.rem(seq, 2)
+    places = near * groups // 2
+    offsets = range(-((steps - 1) // 2), steps - (steps - 1) // 2)
+
+    def at_offset(offset, other):
+        return lax.rem(along + offset + places, places) * 2 + lax.rem(side + other, 2)
+
+    def around_copies(index, offset, other):
+        def outward():
+            return to_dp(tap_near.at[mine], tap_near.at[mine], tn_send.at[index], tn_sem.at[mine], at_offset(-offset, other))
+
+        def inward():
+            slot = lax.rem(at_offset(offset, other), near)
+            return to_dp(tap_near.at[slot], tap_near.at[slot], tn_send.at[index], tn_sem.at[slot], at_offset(offset, other))
+
+        return outward, inward
+
+    around = [
+        around_copies(index, offset, other)
+        for index, (offset, other) in enumerate((o, s) for o in offsets for s in range(2) if (o, s) != (0, 0))
+    ]
+
     barrier = pltpu.get_barrier_semaphore()
 
     def greet_ctx(r, carry):
@@ -139,24 +177,61 @@
     lax.fori_loop(1, n, greet_ctx, 0)
     lax.fori_loop(1, near, greet_near, 0)
     lax.fori_loop(1, groups, greet_far, 0)
+    greeted = [(o, s) for o in sorted(set(offsets) | {-o for o in offsets}) for s in range(2) if (o, s) != (0, 0)]
+    for offset, other in greeted:
+        pl.semaphore_signal(barrier, inc=1, device_id=(at_offset(offset, other), me), device_id_type=MESH)
 
     loads = [
         pltpu.make_async_copy(source, target, in_sem.at[i])
         for i, (source, target) in enumerate([
-            (x_hbm.at[pl.ds(span - ROWS, ROWS), :], x_last), (x_hbm, x_ref),
+            (x_hbm.at[pl.ds(span - ROWS, ROWS), :], x_last),
+            (res_hbm, res_ref), (decay_hbm, decay_ref), (node_hbm, node_ref), (x_hbm, x_ref),
             (letters_hbm, letters_ref), (table_hbm, table_ref), (taps_hbm, taps_ref), (cot_hbm, cot_ref),
-            (mom_hbm, mom_ref), (res_hbm, res_ref), (decay_hbm, decay_ref), (node_hbm, node_ref),
+            (mom_hbm, mom_ref),
             (fwd_hbm, fwd_ref), (inv_hbm, inv_ref), (resp_hbm, resp_ref), (spread_hbm, spread_ref),
         ])
     ]
     for load in loads:
         load.start()
+    for load in loads[1:4]:
+        load.wait()
+    rate, weight = decay_ref[...], res_ref[...]
+    twice = 2.0 * rate
+    series = 1.0 - twice * (1.0 / 7.0)
+    for term in (6.0, 5.0, 4.0, 3.0, 2.0):
+        series = 1.0 - twice * (1.0 / term) * series
+    scale = jnp.sqrt(twice * series)
+    gain = weight * scale
+    par_s[0] = gain
+    par_s[1] = scale
+    node_col = node_ref[...]
+    own_filter = jnp.zeros((NODES, chans), F32)
+    for m in range(MODES):
+        wave = par_s[0, m : m + 1, :] * jnp.exp(-decay_ref[m : m + 1, :] * node_col)
+        gt_s[m] = wave
+        own_filter = own_filter + wave
+    hn_stage[...] = own_filter.astype(BF16)
+    hn_recv[me] = own_filter.astype(BF16)
+
+    for m in range(MODES):
+        gr_s[m] = par_s[0, m : m + 1, :] * jnp.exp(-decay_ref[m : m + 1, :] * (float(span) - node_col))
+    for k in range(NODES):
+        e_s[k] = jnp.exp(-rate * float(nodes[k]))
+        ep_s[k] = jnp.exp(-rate * float(span - nodes[k]))
+
     loads[0].wait()
     halo_stage[...] = x_last[...].astype(F32)[ROWS - 2 :, :]
-    pl.semaphore_wait(barrier, (n - 1) + (near - 1) + (groups - 1))
+    pl.semaphore_wait(barrier, (n - 1) + (near - 1) + (groups - 1) + len(greeted))
     halo = to_ctx(halo_stage, halo_recv, edge_sem.at[0], edge_sem.at[1], ahead)
     halo.start()
-    for load in loads[1:6]:
+
+    def send_filter(r, carry):
+        d = lax.rem(me + r, n)
+        to_ctx(hn_stage, hn_recv.at[me], hn_send.at[d], hn_sem.at[me], d).start()
+        return carry
+
+    lax.fori_loop(1, n, send_filter, 0)
+    for load in loads[4:9]:
         load.wait()
 
     codes = jnp.concatenate([letters_ref[...] + 4 * s for s in range(3)], axis=1)
@@ -198,7 +273,7 @@
         return carry
 
     lax.fori_loop(0, n, late_rows, 0)
-    loads[6].wait()
+    loads[9].wait()
     halo.wait()
     xs[6:8, :] = jnp.where(me > 0, halo_recv[...], 0.0)
 
@@ -218,80 +293,65 @@
     lax.fori_loop(1, sets + 1, node_sums, 0)
     pq_recv[me] = pq_stage[me]
 
-    for load in loads[7:]:
+    for load in loads[10:]:
         load.wait()
-    rate, weight = decay_ref[...], res_ref[...]
-    twice = 2.0 * rate
-    series = 1.0 - twice * (1.0 / 7.0)
-    for term in (6.0, 5.0, 4.0, 3.0, 2.0):
-        series = 1.0 - twice * (1.0 / term) * series
-    scale = jnp.sqrt(twice * series)
-    gain = weight * scale
-    par_s[0] = gain
-    par_s[1] = scale
-    node_col = node_ref[...]
-    own_filter = jnp.zeros((NODES, chans), F32)
-    for m in range(MODES):
-        wave = par_s[0, m : m + 1, :] * jnp.exp(-decay_ref[m : m + 1, :] * node_col)
-        gt_s[m] = wave
-        own_filter = own_filter + wave
-    hn_stage[...] = own_filter.astype(BF16)
-    hn_recv[me] = own_filter.astype(BF16)
-
-    def send_filter(r, carry):
+    inv_s[...] = inv_ref[...].astype(BF16)
+
+    spec_m[...] = dot(fwd_ref[...], mix_s[...])
+    spec_g[...] = dot(fwd_ref[...], gate_s[...])
+
+    def correlate(t, carry):
+        at = pl.ds(pl.multiple_of(t * LANES, LANES), LANES)
+        for c in range(chunks):
+            re, im = slice(c * ROWS, c * ROWS + ROWS), slice(span + c * ROWS, span + c * ROWS + ROWS)
+            mr, mi = spec_m[re, at], spec_m[im, at]
+            gr, gi = spec_g[re, at], spec_g[im, at]
+            prod_s[0, re, at] = (gr * mr + gi * mi).astype(BF16)
+            prod_s[0, im, at] = (gi * mr - gr * mi).astype(BF16)
+        return carry
+
+    lax.fori_loop(0, n * chans // LANES, correlate, 0)
+    both = dot(inv_s[span:, :], prod_s[0])
+    sums = both[:NODES] + both[NODES:]
+    for d in range(n):
+        fgn_stage[d] = sums[:, d * chans : (d + 1) * chans]
+
+    def send_correlation(r, carry):
         d = lax.rem(me + r, n)
-        to_ctx(hn_stage, hn_recv.at[me], hn_send.at[d], hn_sem.at[me], d).start()
-        return carry
-
-    lax.fori_loop(1, n, send_filter, 0)
-    for m in range(MODES):
-        gr_s[m] = par_s[0, m : m + 1, :] * jnp.exp(-decay_ref[m : m + 1, :] * (float(span) - node_col))
-    for k in range(NODES):
-        e_s[k] = jnp.exp(-rate * float(nodes[k]))
-        ep_s[k] = jnp.exp(-rate * float(span - nodes[k]))
-    inv_s[...] = inv_ref[...].astype(BF16)
-
-    def spectra(r, carry):
-        first = first_of(r)
-        at = set_lanes(first)
-        spec_m[:, at] = dot(fwd_ref[...], mix_s[:, at])
-        spec_g[:, at] = dot(fwd_ref[...], gate_s[:, at])
-
-        def multiply(t, carry):
-            some = pl.ds(pl.multiple_of(t * LANES, LANES), LANES)
-            here = pl.ds(pl.multiple_of(first * chans + t * LANES, LANES), LANES)
-            for c in range(chunks):
-                re, im = slice(c * ROWS, c * ROWS + ROWS), slice(span + c * ROWS, span + c * ROWS + ROWS)
-                mr, mi = spec_m[re, here], spec_m[im, here]
-                gr, gi = spec_g[re, here], spec_g[im, here]
-                prod_s[0, re, some] = (gr * mr + gi * mi).astype(BF16)
-                prod_s[0, im, some] = (gi * mr - gr * mi).astype(BF16)
-            return carry
-
-        lax.fori_loop(0, width // LANES, multiply, 0)
-        both = dot(inv_s[span:, :], prod_s[0])
-        sums = both[:NODES] + both[NODES:]
-        for g in range(wide):
-            fgn_stage[first + g] = sums[:, g * chans : (g + 1) * chans]
-        send_others(first, fgn_stage, fgn_recv, fgn_send, fgn_sem)
-        return carry
-
-    lax.fori_loop(1, sets + 1, spectra, 0)
+        to_ctx(fgn_stage.at[d], fgn_recv.at[me], fgn_send.at[d], fgn_sem.at[me], d).start()
+        return carry
+
+    lax.fori_loop(1, n, send_correlation, 0)
+
+    def take_filter(r, carry):
+        d = lax.rem(me + r, n)
+        to_ctx(hn_stage, hn_recv.at[d], hn_send.at[d], hn_sem.at[d], d).wait()
+        return carry
+
+    lax.fori_loop(1, n, take_filter, 0)
+
+    own = jnp.concatenate([hn_recv[d] for d in range(n)], axis=1)
+    spec_h[...] = dot(resp_ref[...], jnp.concatenate([own, own], axis=0))
 
     take_others(pq_stage, pq_recv, pq_send, pq_sem)
 
+    def weigh(buffer, rows, k, table, sums):
+        return [total + buffer[i, rows + k : rows + k + 1, :] * table[k] for i, total in enumerate(sums)]
+
     def states(j, carry):
-        row_s[...] = pq_recv[j].astype(F32)
-        a_sum = jnp.zeros((MODES, chans), F32)
-        r_sum = jnp.zeros((MODES, chans), F32)
+        for i in range(2):
+            row_s[i] = pq_recv[2 * j + i].astype(F32)
+        a_sums = [jnp.zeros((MODES, chans), F32) for _ in range(2)]
+        r_sums = [jnp.zeros((MODES, chans), F32) for _ in range(2)]
         for k in range(NODES):
-            a_sum = a_sum + row_s[k : k + 1, :] * ep_s[k]
-            r_sum = r_sum + row_s[NODES + k : NODES + k + 1, :] * e_s[k]
-        a_s[j] = a_sum
-        r_s[j] = r_sum
-        return carry
-
-    lax.fori_loop(0, n, states, 0)
+            a_sums = weigh(row_s, 0, k, ep_s, a_sums)
+            r_sums = weigh(row_s, NODES, k, e_s, r_sums)
+        for i in range(2):
+            a_s[2 * j + i] = a_sums[i]
+            r_s[2 * j + i] = r_sums[i]
+        return carry
+
+    lax.fori_loop(0, n // 2, states, 0)
     step = jnp.exp(-decay_ref[...] * float(span))
 
     def recur(i, carry):
@@ -304,71 +364,58 @@
     lax.fori_loop(0, n, recur, (nothing, nothing))
 
     def respond(r, carry):
-        d = lax.rem(me + r, n)
-        y_sum = jnp.zeros((NODES, chans), F32)
-        z_sum = jnp.zeros((NODES, chans), F32)
+        pair_of = [lax.rem(me // 2 * 2 + 2 * r + i, n) for i in range(2)]
+        y_sums = [jnp.zeros((NODES, chans), F32) for _ in range(2)]
+        z_sums = [jnp.zeros((NODES, chans), F32) for _ in range(2)]
         for m in range(MODES):
-            y_sum = y_sum + s_s[d, m : m + 1, :] * gt_s[m]
-            z_sum = z_sum + u_s[d, m : m + 1, :] * gr_s[m]
-        yz_stage[d] = jnp.concatenate([y_sum, z_sum], axis=0).astype(BF16)
-
-        @pl.when(r < n)
-        def _():
-            to_ctx(yz_stage.at[d], yz_recv.at[me], yz_send.at[d], yz_sem.at[me], d).start()
-
-        return carry
-
-    lax.fori_loop(1, n + 1, respond, 0)
+            y_sums = [total + s_s[d, m : m + 1, :] * gt_s[m] for d, total in zip(pair_of, y_sums)]
+            z_sums = [total + u_s[d, m : m + 1, :] * gr_s[m] for d, total in zip(pair_of, z_sums)]
+        for i in range(2):
+            yz_stage[pair_of[i]] = jnp.concatenate([y_sums[i], z_sums[i]], axis=0).astype(BF16)
+        for d in pair_of:
+
+            @pl.when(d != me)
+            def _():
+                to_ctx(yz_stage.at[d], yz_recv.at[me], yz_send.at[d], yz_sem.at[me], d).start()
+
+        return carry
+
+    lax.fori_loop(1, n // 2 + 1, respond, 0)
     yz_recv[me] = yz_stage[me]
 
-    def take_filter(r, carry):
-        d = lax.rem(me + r, n)
-        to_ctx(hn_stage, hn_recv.at[d], hn_send.at[d], hn_sem.at[d], d).wait()
-        return carry
-
-    lax.fori_loop(1, n, take_filter, 0)
-
-    def inside(r, carry):
-        first = first_of(r)
-        at = set_lanes(first)
-        own = jnp.concatenate([hn_recv[first + g] for g in range(wide)], axis=1)
-        spec_h[...] = dot(resp_ref[...], jnp.concatenate([own, own], axis=0))
-
-        def multiply(t, carry):
-            some = pl.ds(pl.multiple_of(t * LANES, LANES), LANES)
-            here = pl.ds(pl.multiple_of(first * chans + t * LANES, LANES), LANES)
-            for c in range(chunks):
-                re, im = slice(c * ROWS, c * ROWS + ROWS), slice(span + c * ROWS, span + c * ROWS + ROWS)
-                hr, hi = spec_h[re, some], spec_h[im, some]
-                mr, mi = spec_m[re, here], spec_m[im, here]
-                gr, gi = spec_g[re, here], spec_g[im, here]
-                prod_s[0, re, some] = (hr * mr - hi * mi).astype(BF16)
-                prod_s[0, im, some] = (hr * mi + hi * mr).astype(BF16)
-                prod_s[1, re, some] = (hr * gr + hi * gi).astype(BF16)
-                prod_s[1, im, some] = (hr * gi - hi * gr).astype(BF16)
-            return carry
-
-        lax.fori_loop(0, width // LANES, multiply, 0)
-        conv_s[:, at] = dot(inv_s[:span, :], prod_s[0])
-        back_s[:, at] = dot(inv_s[:span, :], prod_s[1])
-        return carry
-
-    lax.fori_loop(1, sets + 1, inside, 0)
+    def inside(t, carry):
+        at = pl.ds(pl.multiple_of(t * LANES, LANES), LANES)
+        for c in range(chunks):
+            re, im = slice(c * ROWS, c * ROWS + ROWS), slice(span + c * ROWS, span + c * ROWS + ROWS)
+            hr, hi = spec_h[re, at], spec_h[im, at]
+            mr, mi = spec_m[re, at], spec_m[im, at]
+            gr, gi = spec_g[re, at], spec_g[im, at]
+            prod_s[0, re, at] = (hr * mr - hi * mi).astype(BF16)
+            prod_s[0, im, at] = (hr * mi + hi * mr).astype(BF16)
+            prod_s[1, re, at] = (hr * gr + hi * gi).astype(BF16)
+            prod_s[1, im, at] = (hr * gi - hi * gr).astype(BF16)
+        return carry
+
+    lax.fori_loop(0, n * chans // LANES, inside, 0)
+    conv_s[...] = dot(inv_s[:span, :], prod_s[0])
+    back_s[...] = dot(inv_s[:span, :], prod_s[1])
 
     def lags(j, carry):
-        sums = pq_recv[j].astype(F32)
-        row_s[:NODES] = sums[:NODES] * (float(span) - node_ref[...])
-        row_s[NODES:] = sums[NODES:] * node_ref[...]
-        a_sum = jnp.zeros((MODES, chans), F32)
-        r_sum = jnp.zeros((MODES, chans), F32)
+        for i in range(2):
+            sums = pq_recv[2 * j + i].astype(F32)
+            row_s[i, :NODES] = sums[:NODES] * (float(span) - node_ref[...])
+            row_s[i, NODES:] = sums[NODES:] * node_ref[...]
+        a_sums = [jnp.zeros((MODES, chans), F32) for _ in range(2)]
+        r_sums = [jnp.zeros((MODES, chans), F32) for _ in range(2)]
         for k in range(NODES):
-            a_sum = a_sum + row_s[k : k + 1, :] * ep_s[k]
-            r_sum = r_sum + row_s[NODES + k : NODES + k + 1, :] * e_s[k]
-        al_s[j] = a_sum
-        rl_s[j] = r_sum
-        return carry
-
-    lax.fori_loop(0, n, lags, 0)
+            a_sums = weigh(row_s, 0, k, ep_s, a_sums)
+            r_sums = weigh(row_s, NODES, k, e_s, r_sums)
+        for i in range(2):
+            al_s[2 * j + i] = a_sums[i]
+            rl_s[2 * j + i] = r_sums[i]
+        return carry
+
+    lax.fori_loop(0, n // 2, lags, 0)
 
     def pair(i, carry):
         lag_state, exp_sum, lag_sum = carry
@@ -383,11 +430,11 @@
     near_sum = fgn_recv[0]
     for d in range(1, n):
         near_sum = near_sum + fgn_recv[d]
-    row_s[:NODES] = near_sum
-    row_s[NODES:] = near_sum * node_ref[...]
+    row_s[0, :NODES] = near_sum
+    row_s[0, NODES:] = near_sum * node_ref[...]
     for k in range(NODES):
-        exp_sum = exp_sum + row_s[k : k + 1, :] * e_s[k]
-        lag_sum = lag_sum + row_s[NODES + k : NODES + k + 1, :] * e_s[k]
+        exp_sum = exp_sum + row_s[0, k : k + 1, :] * e_s[k]
+        lag_sum = lag_sum + row_s[0, NODES + k : NODES + k + 1, :] * e_s[k]
     mode_grads = (
         par_s[1] * exp_sum,
         res_ref[...] * jnp.exp(-2.0 * decay_ref[...]) / par_s[1] * exp_sum - par_s[0] * lag_sum,
@@ -444,19 +491,14 @@
     send_near(lambda p: mode_stage.at[p], mode_one, mo_send, mo_sem)
     mode_one[mine] = mode_stage[mine]
 
+    take_others(yz_stage, yz_recv, yz_send, yz_sem)
+    for which in range(2):
+        rows = slice(which * NODES, (which + 1) * NODES)
+        node = jnp.concatenate([yz_recv[d, rows] for d in range(n)], axis=1)
+        far_s[which] = dot(spread_ref[...], jnp.concatenate([node, node], axis=0))
+
     def finish(r, carry):
         first = first_of(r)
-        for g in range(wide):
-            d = first + g
-
-            @pl.when(d != me)
-            def _():
-                to_ctx(yz_stage.at[d], yz_recv.at[d], yz_send.at[d], yz_sem.at[d], d).wait()
-
-        y_node = jnp.concatenate([yz_recv[first + g, :NODES] for g in range(wide)], axis=1)
-        z_node = jnp.concatenate([yz_recv[first + g, NODES:] for g in range(wide)], axis=1)
-        far_s[0] = dot(spread_ref[...], jnp.concatenate([y_node, y_node], axis=0))
-        far_s[1] = dot(spread_ref[...], jnp.concatenate([z_node, z_node], axis=0))
 
         def gradients(g, carry):
             for t in range(chans // LANES):
@@ -466,8 +508,8 @@
                 for c in range(chunks):
                     low = c * ROWS
                     rows = slice(low, low + ROWS)
-                    conv = (conv_s[rows, at] + far_s[0, rows, some]).astype(BF16).astype(F32)
-                    back = (back_s[rows, at] + far_s[1, rows, some]).astype(BF16).astype(F32)
+                    conv = (conv_s[rows, at] + far_s[0, rows, at]).astype(BF16).astype(F32)
+                    back = (back_s[rows, at] + far_s[1, rows, at]).astype(BF16).astype(F32)
                     conv_s[rows, at] = conv
                     back_s[rows, at] = back
                     grads = [
@@ -482,16 +524,15 @@
                             part = grads[s] * lag[j]
                             totals[3 * s + j] = totals[3 * s + j] + (part[:8] + part[8:])
                 for i in range(9):
-                    piece_stage[first + g, 12 + i : 13 + i, t * LANES : (t + 1) * LANES] = jnp.sum(
-                        totals[i], axis=0, keepdims=True
-                    )
+                    sums_s[g, 12 + i : 13 + i, t * LANES : (t + 1) * LANES] = jnp.sum(totals[i], axis=0, keepdims=True)
             return carry
 
         lax.fori_loop(0, wide, gradients, 0)
         letter_sums = dot(hot_t[...], fg_s[...])
         for g in range(wide):
-            piece_stage[first + g, :12, :] = letter_sums[:12, g * chans : (g + 1) * chans]
-            piece_stage[first + g, 21:, :] = jnp.zeros((PIECE - 21, chans), F32)
+            sums_s[g, :12, :] = letter_sums[:12, g * chans : (g + 1) * chans]
+            sums_s[g, 21:, :] = jnp.zeros((PIECE - 21, chans), F32)
+            piece_stage[first + g] = packed(sums_s[g])
         send_others(first, piece_stage, piece_recv, piece_send, piece_sem)
         return carry
 
@@ -503,8 +544,11 @@
 
     take_others(piece_stage, piece_recv, piece_send, piece_sem)
     piece_recv[me] = piece_stage[me]
-    tap_near[mine] = sum_of(piece_recv)
-    send_near(lambda p: tap_near.at[mine], tap_near, tn_send, tn_sem)
+    piece = piece_recv[0].astype(F32)
+    for d in range(1, n):
+        piece = piece + piece_recv[d].astype(F32)
+    tap_far[block] = unpacked(piece)
+    send_far(tap_far, tf_send, tf_sem)
 
     w_s[0, span : span + 8, :] = jnp.zeros((8, chans), F32)
     w_s[1, span : span + 8, :] = jnp.zeros((8, chans), F32)
@@ -542,10 +586,6 @@
     main = pltpu.make_async_copy(grad_ref.at[body, :], grad_hbm.at[body, :], out_sem.at[0])
     main.start()
 
-    take_near(tap_near, tn_send, tn_sem)
-    tap_far[block] = sum_of(tap_near)
-    send_far(tap_far, tf_send, tf_sem)
-
     edge.wait()
     tail_s[ROWS - 2 :, :] = tail_s[ROWS - 2 :, :] + jnp.where(me < n - 1, edge_recv[...], 0.0)
     grad_ref[span - ROWS :, :] = tail_s[...].astype(BF16)
@@ -556,6 +596,10 @@
     take_far(mode_two, mt_send, mt_sem)
     mode_three[mine] = sum_of(mode_two)
     send_near(lambda p: mode_three.at[mine], mode_three, mh_send, mh_sem)
+    take_far(tap_far, tf_send, tf_sem)
+    tap_near[mine] = sum_of(tap_far)
+    for copy, _ in around:
+        copy().start()
     main.wait()
     tail.wait()
     take_near(mode_three, mh_send, mh_sem)
@@ -563,8 +607,9 @@
         which, row, lane, slot, place = tile_of(index)
         row = PIECE + which * MODES + row
         total_ref[row : row + 8, lane : lane + LANES] = mode_three[slot, place : place + 8, :]
-    take_far(tap_far, tf_send, tf_sem)
-    total_ref[:PIECE, :] = sum_of(tap_far)
+    for _, copy in around:
+        copy().wait()
+    total_ref[:PIECE, :] = sum_of(tap_near)
 
 
 def hand_out(total_ref, grad_ref, grad_out, taps_out, table_out, res_out, decay_out):
@@ -608,14 +653,15 @@
         pltpu.VMEM((ROWS, width), F32),
         pltpu.VMEM((2 * span, width), F32),
         pltpu.VMEM((2 * span, width), F32),
-        pltpu.VMEM((2 * span, several), F32),
-        pltpu.VMEM((2, 2 * span, several), BF16),
-        pltpu.VMEM((2, span, several), F32),
+        pltpu.VMEM((2 * span, width), F32),
+        pltpu.VMEM((2, 2 * span, width), BF16),
+        pltpu.VMEM((2, span, width), F32),
         pltpu.VMEM((3 * span, several), BF16),
+        pltpu.VMEM((wide, PIECE, chans), F32),
         pltpu.VMEM((2, span + 8, chans), F32),
         pltpu.VMEM((ROWS, width), F32),
     ] + [pltpu.VMEM((NODES, MODES, chans), F32)] * 4 + [pltpu.VMEM((n, MODES, chans), F32)] * 6 + [
-        pltpu.VMEM((2 * NODES, chans), F32),
+        pltpu.VMEM((2, 2 * NODES, chans), F32),
         pltpu.VMEM((2, MODES, chans), F32),
     ] + [pltpu.VMEM((2, width), F32)] * 4 + [
         pltpu.VMEM((NODES, chans), BF16),
@@ -626,8 +672,8 @@
         pltpu.VMEM((n, NODES, chans), F32),
         pltpu.VMEM((n, 2 * NODES, chans), BF16),
         pltpu.VMEM((n, 2 * NODES, chans), BF16),
-        pltpu.VMEM((n, PIECE, chans), F32),
-        pltpu.VMEM((n, PIECE, chans), F32),
+        pltpu.VMEM((n, 16, chans * 3 // 2), BF16),
+        pltpu.VMEM((n, 16, chans * 3 // 2), BF16),
         pltpu.VMEM((near, share, LANES), F32),
         pltpu.VMEM((near, share, LANES), F32),
         pltpu.VMEM((groups, share, LANES), F32),

time: 64.5 us -> 59.4 us (0.921)
  Pallas kernels: 63.7 us -> 58.3 us
    pallas_call x1, Pallas kernels: 61.4 us -> 56 us  [shards(): pl.pallas_call(functools.partial(kernel, n, near, groups, wide, span, cha...]
where the time goes in v1:
time: 59.4 us; the launch traced here: 59 us
  Pallas kernels  58.3 us (98%)
  between operations  0.64 us (1%)
    pallas_call x1, Pallas kernels, shards(): pl.pallas_call(functools.partial(kernel, n, near, groups, wide, span, cha...  56 us
    pallas_call x1, Pallas kernels, shards(): pl.pallas_call(hand_out, out_shape=(jax.ShapeDtypeStruct((span, width), B...  2.31 us

profile of v1, /device:TPU:1, one launch (start us, length us, event | category | flops | bytes accessed | tf_op | source)
XLA Modules:
  0.0 59.0 jit_solution(8647967542278372842)
XLA Ops:
  0.6 56.0 %shard_map.164 = (bf16[128,4096]{1,0:T(8,128)(2,1)}, f32[56,256]{1,0:T(8,128)}) custom-call(bf16[128,4096]{1,0:T(8,128)(2,1)} %bitcast.7, s32[1,128]{1,0:T(1,128)} %refs_1_.1, bf16[3,4,4096]{2,1,0:T(4,128)(2,1)} %refs_2_.1, bf16[3,3,4096]{2,1,0:T(4,128)(2,1)} %refs_3_.1, f32[16,256]{1,0:T(8,128)} %bitcast.9, f32[16,256]{1,0:T(8,128)} %bitcast.10, ...), custom_call_target="tpu_custom_call" | custom-call | tf_op jit(solution)/shard_map/pallas_call | solution.py:687
  56.7 2.3 %shard_map.165 = (bf16[128,4096]{1,0:T(8,128)(2,1)}, f32[3,3,256]{2,1,0:T(4,128)}, f32[3,4,256]{2,1,0:T(4,128)}, f32[16,256]{1,0:T(8,128)}, f32[16,256]{1,0:T(8,128)}) custom-call(f32[56,256]{1,0:T(8,128)} %get-tuple-element.12.total_ref, bf16[128,4096]{1,0:T(8,128)(2,1)} %get-tuple-element.13.grad_ref), custom_call_target="tpu_custom_call" | custom-call | tf_op jit(solution)/shard_map/pallas_call | solution.py:700

commit v2 on v1

--- a/solution.py
+++ b/solution.py
@@ -104,8 +104,13 @@
     def set_lanes(first):
         return pl.ds(pl.multiple_of(first * chans, width), width)
 
+    def across(position, r, count):
+        side_size = count // 2
+        side = lax.rem(position // side_size + 1 - (r - 1) // side_size, 2)
+        return side * side_size + lax.rem(position + r, side_size)
+
     def first_of(r):
-        return lax.rem(me // wide + r, sets) * wide
+        return across(me // wide, r, sets) * wide if sets > 1 else 0
 
     def to_ctx(source, target, send, recv, d):
         return pltpu.make_async_remote_copy(
@@ -155,7 +160,7 @@
 
     around = [
         around_copies(index, offset, other)
-        for index, (offset, other) in enumerate((o, s) for o in offsets for s in range(2) if (o, s) != (0, 0))
+        for index, (offset, other) in enumerate((o, s) for o in sorted(offsets, key=abs, reverse=True) for s in (1, 0) if (o, s) != (0, 0))
     ]
 
     barrier = pltpu.get_barrier_semaphore()
@@ -364,7 +369,7 @@
     lax.fori_loop(0, n, recur, (nothing, nothing))
 
     def respond(r, carry):
-        pair_of = [lax.rem(me // 2 * 2 + 2 * r + i, n) for i in range(2)]
+        pair_of = [2 * across(me // 2, r, n // 2) + i if n > 2 else i for i in range(2)]
         y_sums = [jnp.zeros((NODES, chans), F32) for _ in range(2)]
         z_sums = [jnp.zeros((NODES, chans), F32) for _ in range(2)]
         for m in range(MODES):
@@ -597,7 +602,7 @@
     mode_three[mine] = sum_of(mode_two)
     send_near(lambda p: mode_three.at[mine], mode_three, mh_send, mh_sem)
     take_far(tap_far, tf_send, tf_sem)
-    tap_near[mine] = sum_of(tap_far)
+    tap_near[mine] = packed(sum_of(tap_far))
     for copy, _ in around:
         copy().start()
     main.wait()
@@ -609,7 +614,10 @@
         total_ref[row : row + 8, lane : lane + LANES] = mode_three[slot, place : place + 8, :]
     for _, copy in around:
         copy().wait()
-    total_ref[:PIECE, :] = sum_of(tap_near)
+    total = tap_near[0].astype(F32)
+    for p in range(1, near):
+        total = total + tap_near[p].astype(F32)
+    total_ref[:PIECE, :] = unpacked(total)
 
 
 def hand_out(total_ref, grad_ref, grad_out, taps_out, table_out, res_out, decay_out):
@@ -678,7 +686,7 @@
         pltpu.VMEM((near, share, LANES), F32),
         pltpu.VMEM((groups, share, LANES), F32),
         pltpu.VMEM((near, share, LANES), F32),
-        pltpu.VMEM((near, PIECE, chans), F32),
+        pltpu.VMEM((near, 16, chans * 3 // 2), BF16),
         pltpu.VMEM((groups, PIECE, chans), F32),
         dma((len(operands) + 1,)),
         dma((2,)),

time: 59.4 us -> 58.8 us (0.990)
  no operation moved by 1% of the time
where the time goes in v2:
time: 58.8 us; the launch traced here: 58.6 us
  Pallas kernels  58 us (99%)
  between operations  0.64 us (1%)
    pallas_call x1, Pallas kernels, shards(): pl.pallas_call(functools.partial(kernel, n, near, groups, wide, span, cha...  55.7 us
    pallas_call x1, Pallas kernels, shards(): pl.pallas_call(hand_out, out_shape=(jax.ShapeDtypeStruct((span, width), B...  2.31 us

profile of v2, /device:TPU:1, one launch (start us, length us, event | category | flops | bytes accessed | tf_op | source)
XLA Modules:
  0.0 58.6 jit_solution(12578522149075481804)
XLA Ops:
  0.6 55.7 %shard_map.164 = (bf16[128,4096]{1,0:T(8,128)(2,1)}, f32[56,256]{1,0:T(8,128)}) custom-call(bf16[128,4096]{1,0:T(8,128)(2,1)} %bitcast.7, s32[1,128]{1,0:T(1,128)} %refs_1_.1, bf16[3,4,4096]{2,1,0:T(4,128)(2,1)} %refs_2_.1, bf16[3,3,4096]{2,1,0:T(4,128)(2,1)} %refs_3_.1, f32[16,256]{1,0:T(8,128)} %bitcast.9, f32[16,256]{1,0:T(8,128)} %bitcast.10, ...), custom_call_target="tpu_custom_call" | custom-call | tf_op jit(solution)/shard_map/pallas_call | solution.py:695
  56.3 2.3 %shard_map.165 = (bf16[128,4096]{1,0:T(8,128)(2,1)}, f32[3,3,256]{2,1,0:T(4,128)}, f32[3,4,256]{2,1,0:T(4,128)}, f32[16,256]{1,0:T(8,128)}, f32[16,256]{1,0:T(8,128)}) custom-call(f32[56,256]{1,0:T(8,128)} %get-tuple-element.12.total_ref, bf16[128,4096]{1,0:T(8,128)(2,1)} %get-tuple-element.13.grad_ref), custom_call_target="tpu_custom_call" | custom-call | tf_op jit(solution)/shard_map/pallas_call | solution.py:708

commit v3 on v2

--- a/solution.py
+++ b/solution.py
@@ -165,27 +165,6 @@
 
     barrier = pltpu.get_barrier_semaphore()
 
-    def greet_ctx(r, carry):
-        pl.semaphore_signal(barrier, inc=1, device_id=(seq, lax.rem(me + r, n)), device_id_type=MESH)
-        return carry
-
-    def greet_near(r, carry):
-        peer = block * near + lax.rem(mine + r, near)
-        pl.semaphore_signal(barrier, inc=1, device_id=(peer, me), device_id_type=MESH)
-        return carry
-
-    def greet_far(r, carry):
-        peer = lax.rem(block + r, groups) * near + mine
-        pl.semaphore_signal(barrier, inc=1, device_id=(peer, me), device_id_type=MESH)
-        return carry
-
-    lax.fori_loop(1, n, greet_ctx, 0)
-    lax.fori_loop(1, near, greet_near, 0)
-    lax.fori_loop(1, groups, greet_far, 0)
-    greeted = [(o, s) for o in sorted(set(offsets) | {-o for o in offsets}) for s in range(2) if (o, s) != (0, 0)]
-    for offset, other in greeted:
-        pl.semaphore_signal(barrier, inc=1, device_id=(at_offset(offset, other), me), device_id_type=MESH)
-
     loads = [
         pltpu.make_async_copy(source, target, in_sem.at[i])
         for i, (source, target) in enumerate([
@@ -198,6 +177,28 @@
     ]
     for load in loads:
         load.start()
+
+    def greet_ctx(r, carry):
+        pl.semaphore_signal(barrier, inc=1, device_id=(seq, lax.rem(me + r, n)), device_id_type=MESH)
+        return carry
+
+    def greet_near(r, carry):
+        peer = block * near + lax.rem(mine + r, near)
+        pl.semaphore_signal(barrier, inc=1, device_id=(peer, me), device_id_type=MESH)
+        return carry
+
+    def greet_far(r, carry):
+        peer = lax.rem(block + r, groups) * near + mine
+        pl.semaphore_signal(barrier, inc=1, device_id=(peer, me), device_id_type=MESH)
+        return carry
+
+    lax.fori_loop(1, n, greet_ctx, 0)
+    lax.fori_loop(1, near, greet_near, 0)
+    lax.fori_loop(1, groups, greet_far, 0)
+    greeted = [(o, s) for o in sorted(set(offsets) | {-o for o in offsets}) for s in range(2) if (o, s) != (0, 0)]
+    for offset, other in greeted:
+        pl.semaphore_signal(barrier, inc=1, device_id=(at_offset(offset, other), me), device_id_type=MESH)
+
     for load in loads[1:4]:
         load.wait()
     rate, weight = decay_ref[...], res_ref[...]

time: 58.8 us -> 58.8 us (level)
  no operation moved by 1% of the time
where the time goes in v3:
time: 58.8 us; the launch traced here: 58.6 us
  Pallas kernels  57.9 us (98%)
  between operations  0.64 us (1%)
    pallas_call x1, Pallas kernels, shards(): pl.pallas_call(functools.partial(kernel, n, near, groups, wide, span, cha...  55.6 us
    pallas_call x1, Pallas kernels, shards(): pl.pallas_call(hand_out, out_shape=(jax.ShapeDtypeStruct((span, width), B...  2.31 us

profile of v3, /device:TPU:1, one launch (start us, length us, event | category | flops | bytes accessed | tf_op | source)
XLA Modules:
  0.0 58.6 jit_solution(10303358739240514910)
XLA Ops:
  0.6 55.6 %shard_map.164 = (bf16[128,4096]{1,0:T(8,128)(2,1)}, f32[56,256]{1,0:T(8,128)}) custom-call(bf16[128,4096]{1,0:T(8,128)(2,1)} %bitcast.7, s32[1,128]{1,0:T(1,128)} %refs_1_.1, bf16[3,4,4096]{2,1,0:T(4,128)(2,1)} %refs_2_.1, bf16[3,3,4096]{2,1,0:T(4,128)(2,1)} %refs_3_.1, f32[16,256]{1,0:T(8,128)} %bitcast.9, f32[16,256]{1,0:T(8,128)} %bitcast.10, ...), custom_call_target="tpu_custom_call" | custom-call | tf_op jit(solution)/shard_map/pallas_call | solution.py:696
  56.2 2.3 %shard_map.165 = (bf16[128,4096]{1,0:T(8,128)(2,1)}, f32[3,3,256]{2,1,0:T(4,128)}, f32[3,4,256]{2,1,0:T(4,128)}, f32[16,256]{1,0:T(8,128)}, f32[16,256]{1,0:T(8,128)}) custom-call(f32[56,256]{1,0:T(8,128)} %get-tuple-element.12.total_ref, bf16[128,4096]{1,0:T(8,128)(2,1)} %get-tuple-element.13.grad_ref), custom_call_target="tpu_custom_call" | custom-call | tf_op jit(solution)/shard_map/pallas_call | solution.py:709
